TPU v7x, 256 devices: a whole 4x4x8 slice. The times are simulated.
256 devices in a mesh: head: 8 (over x, core), ctx: 32 (over z, y).
Axes of the slice: x: 4, y: 4, z: 8, core: 2. Of those that a mesh axis runs over, the one named last changes fastest.
Arguments:
- queries: bfloat16 [32, 1024, 8192], P('ctx', 'head'), may hold values from -9 to 9
- segment_kv: bfloat16 [32, 1024, 2048], P('ctx', 'head'), may hold values from -9 to 9
- cache_kv: bfloat16 [131072, 2048], P('ctx', 'head'), may hold values from -6 to 6
- vertical_ids: int32 [8, 32, 2], P('head', 'ctx'), may hold values from 0 to 47, as said below
- vertical_counts: int32 [8, 32], P('head'), may hold values from 1 to 2, as said below
- vertical_heads: int32 [64, 64], P('head'), may hold values from 0 to 1, as said below
- slash_offsets: int32 [64, 4], P('head'), may hold values from 0 to 15, as said below
- slash_counts: int32 [64], P('head'), may hold values from 1 to 4
Outputs:
- attended: bfloat16 [32, 1024, 8192], P('ctx', 'head')
Inputs may be any that keep to these rules, and one draw needn't show every extreme that they name: `vertical_ids`: block numbers within one context shard's prefix; the 2 slots of one KV head and shard hold distinct blocks. `vertical_counts`: some shard of each KV head has all 2 slots live. `vertical_heads`: marks stand only on live slots; a head marks at most 8 slots, and some head exactly 8. `slash_offsets`: slot 0 holds 0; the offsets of one head are distinct.
All inputs are finite; a program needn't handle non-finite values.
Results may differ from a plain program's by a relative error of at most 0.0043.
Values may be sent and summed in bfloat16 or wider, within the bound.
A program may use at most 128 MiB of HBM per device.

v0:
```python
import jax
import jax.numpy as jnp
from jax import lax
from jax.sharding import PartitionSpec as P

HEAD_WIDTH = 128
BLOCK_POSITIONS = 64


NEG_FILL = -1e30


def shifted(block, axis, distance):
    devices = range(lax.axis_size(axis))
    route = [((i - distance) % len(devices), i) for i in devices]
    return lax.ppermute(block, axis, route)


def per_device(
    queries,
    segment_kv,
    cache_kv,
    vertical_ids,
    vertical_counts,
    vertical_heads,
    slash_offsets,
    slash_counts,
):
    ctx_size = lax.axis_size("ctx")
    ctx_place = lax.axis_index("ctx")
    q_local, kv_local = (
        lax.all_to_all(queries, "head", split_axis=2, concat_axis=1, tiled=True),
        lax.all_to_all(segment_kv, "head", split_axis=2, concat_axis=1, tiled=True),
    )
    shard_rows = q_local.shape[1]
    heads_here = q_local.shape[2] // HEAD_WIDTH
    kvheads_here = kv_local.shape[2] // (2 * HEAD_WIDTH)
    group_size = heads_here // kvheads_here
    qblocks = shard_rows // BLOCK_POSITIONS
    tail_rows = (qblocks - 1) * BLOCK_POSITIONS
    prefix_rows = cache_kv.shape[0]
    slot_count = vertical_ids.shape[2]
    slash_width = slash_offsets.shape[1]
    seg_rows = kv_local.reshape(shard_rows, kvheads_here, 2 * HEAD_WIDTH)
    pre_rows = cache_kv.reshape(prefix_rows, kvheads_here, 2 * HEAD_WIDTH)
    pre_blocks = pre_rows.reshape(
        prefix_rows // BLOCK_POSITIONS, BLOCK_POSITIONS, kvheads_here, 2 * HEAD_WIDTH
    )
    kv_index = jnp.arange(kvheads_here, dtype=jnp.int32)
    picked = pre_blocks[vertical_ids[:, 0, :], :, kv_index[:, None], :]
    pool_blocks = lax.all_gather(picked, "ctx", axis=1, tiled=True)
    send_tail = jnp.where(
        ctx_place == ctx_size - 1,
        pre_rows[prefix_rows - tail_rows :],
        seg_rows[shard_rows - tail_rows :],
    )
    got_tail = shifted(send_tail, "ctx", 1)
    band_blocks = jnp.concatenate([got_tail, seg_rows], axis=0).reshape(
        2 * qblocks - 1, BLOCK_POSITIONS, kvheads_here, 2 * HEAD_WIDTH
    )
    score_scale = HEAD_WIDTH ** (-0.5)
    columns = ctx_size * slot_count
    slot_ids = jnp.arange(slot_count, dtype=jnp.int32)
    live_slots = (slot_ids[None, None, :] < vertical_counts[:, :, None]).reshape(
        kvheads_here, columns
    )
    head_rows = q_local.reshape(shard_rows, heads_here, HEAD_WIDTH).transpose(1, 0, 2)
    positions = jnp.arange(BLOCK_POSITIONS, dtype=jnp.int32)
    causal = positions[None, :] <= positions[:, None]
    block_ids = jnp.arange(qblocks, dtype=jnp.int32)

    def one_head(inputs):
        rows_in, member, offsets, slash_count, head_index = inputs
        kv_pick = head_index // group_size
        head_band = jnp.take(band_blocks, kv_pick, axis=2)
        head_pool = jnp.take(pool_blocks, kv_pick, axis=0)
        flagged_blocks = (member == 1) & jnp.take(live_slots, kv_pick, axis=0)
        wanted = ctx_size * slot_count // 8
        sorted_order = jnp.argsort(jnp.where(flagged_blocks, 0, 1), stable=True)[:wanted]
        flagged_blocks = flagged_blocks[sorted_order]
        head_pool = head_pool[sorted_order]
        column_key_rows = head_pool[:, :, :HEAD_WIDTH].reshape(-1, HEAD_WIDTH)
        column_value_rows = head_pool[:, :, HEAD_WIDTH:].reshape(-1, HEAD_WIDTH)
        vert_keep = jnp.repeat(flagged_blocks, BLOCK_POSITIONS)[None, :]
        vert_scores = (
            jnp.einsum("qd,kd->qk", rows_in, column_key_rows, preferred_element_type=jnp.float32)
            * score_scale
        )
        band_index = block_ids[:, None] + qblocks - 1 - offsets[None, :]
        slash_kv = head_band[band_index]
        q_blocks = rows_in.reshape(qblocks, BLOCK_POSITIONS, HEAD_WIDTH)
        slash_scores = (
            jnp.einsum(
                "gqd,gskd->gqsk",
                q_blocks,
                slash_kv[..., :HEAD_WIDTH],
                preferred_element_type=jnp.float32,
            )
            * score_scale
        )
        slash_live = jnp.arange(slash_width, dtype=jnp.int32) < slash_count
        slash_keep = slash_live[None, None, :, None] & (
            (offsets > 0)[None, None, :, None] | causal[None, :, None, :]
        )
        vert_max = jnp.max(jnp.where(vert_keep, vert_scores, NEG_FILL), axis=1)
        slash_max = jnp.max(jnp.where(slash_keep, slash_scores, NEG_FILL), axis=(2, 3)).reshape(
            shard_rows
        )
        row_max = jnp.maximum(vert_max, slash_max)
        vert_weights = jnp.where(vert_keep, jnp.exp(vert_scores - row_max[:, None]), 0.0)
        slash_weights = jnp.where(
            slash_keep,
            jnp.exp(slash_scores - row_max.reshape(qblocks, BLOCK_POSITIONS)[:, :, None, None]),
            0.0,
        )
        row_total = jnp.sum(vert_weights, axis=1) + jnp.sum(slash_weights, axis=(2, 3)).reshape(
            shard_rows
        )
        summed = jnp.dot(
            vert_weights.astype(jnp.bfloat16), column_value_rows, preferred_element_type=jnp.float32
        )
        summed = summed + jnp.einsum(
            "gqsk,gskd->gqd",
            slash_weights.astype(jnp.bfloat16),
            slash_kv[..., HEAD_WIDTH:],
            preferred_element_type=jnp.float32,
        ).reshape(shard_rows, HEAD_WIDTH)
        return (summed / row_total[:, None]).astype(jnp.bfloat16)

    attended = lax.map(
        one_head,
        (
            head_rows,
            vertical_heads,
            slash_offsets,
            slash_counts,
            jnp.arange(heads_here, dtype=jnp.int32),
        ),
    )
    outgoing = attended.transpose(1, 0, 2).reshape(1, shard_rows, heads_here * HEAD_WIDTH)
    return lax.all_to_all(outgoing, "head", split_axis=1, concat_axis=2, tiled=True)


def solution(mesh):
    in_specs = (
        P("ctx", "head", None),
        P("ctx", "head", None),
        P("ctx", "head"),
        P("head", "ctx", None),
        P("head", None),
        P("head", None),
        P("head", None),
        P("head"),
    )
    out_specs = P("ctx", "head", None)
    return jax.shard_map(
        per_device, mesh=mesh, in_specs=in_specs, out_specs=out_specs, check_vma=False
    )
```

profile of v0, /device:TPU:1, one launch (start us, length us, event | category | flops | bytes accessed | tf_op | source)
XLA Modules:
  0.0 412.4 jit_solution(2726741583834426988)
XLA Ops:
  7.5 2.8 gather_fusion.3
  10.3 2.4 copy.58
  13.2 12.4 %reduce.3 = bf16[2048,128]{1,0:T(8,128)(2,1)} reduce(bf16[2048,1,128]{2,1,0:T(2,128)(2,1)S(1)} %bitcast.120, bf16[]{:T(256)} %broadcast.358), dimensions={1}, to_apply=%bitcast.63.reduce_sub_computation | reduce | bytes 1048578
  27.6 7.3 %all-to-all-start.1 = ((bf16[8,2,16384]{2,1,0:T(2,128)(2,1)}), bf16[8,2,16384]{2,1,0:T(2,128)(2,1)}, u32[]{:S(2)}, u32[]{:S(2)}) async-start(bf16[8,2,16384]{2,1,0:T(2,128)(2,1)} %reshape.379), calls=%async_computation.1 | async-start | bytes 1048576 | tf_op jit(solution)/shard_map/all_to_all | solution.py:33
  34.9 6.8 %copy.55 = bf16[1,128,8192]{1,0,2:T(2,128)(2,1)} copy(bf16[1,128,8192]{2,1,0:T(8,128)(2,1)S(1)} %copy-done.2) | data formatting | bytes 4194304 | tf_op args[0]
  41.7 45.2 %reduce.2 = bf16[8192,128]{1,0:T(8,128)(2,1)S(1)} reduce(bf16[8192,1,128]{2,1,0:T(2,128)(2,1)} %bitcast.110, bf16[]{:T(256)} %broadcast.358), dimensions={1}, to_apply=%bitcast.61.reduce_sub_computation | reduce | bytes 4194306
  86.9 3.2 reshape.377
  90.1 4.8 %all-to-all-start = ((bf16[8,2,65536]{2,1,0:T(2,128)(2,1)}), bf16[8,2,65536]{2,1,0:T(2,128)(2,1)S(1)}, u32[]{:S(2)}, u32[]{:S(2)}) async-start(bf16[8,2,65536]{2,1,0:T(2,128)(2,1)} %reshape.377), calls=%async_computation | async-start | bytes 4194304 | tf_op jit(solution)/shard_map/all_to_all | solution.py:32
  95.0 2.2 reshape.380
  101.3 18.3 %collective-permute-done = bf16[960,1,256]{2,0,1:T(8,128)(2,1)S(1)} collective-permute-done((bf16[960,1,256]{2,0,1:T(8,128)(2,1)}, bf16[960,1,256]{2,0,1:T(8,128)(2,1)S(1)}, u32[]{:S(2)}, u32[]{:S(2)}) %collective-permute-start) | collective-permute-done | bytes 491552 | tf_op jit(solution)/shard_map/ppermute | solution.py:16
  121.3 4.4 %reshape.378 = bf16[8192,1,128]{2,1,0:T(2,128)(2,1)} reshape(bf16[8,2,65536]{2,1,0:T(2,128)(2,1)S(1)} %all-to-all-done) | data formatting | bytes 4194304
  125.7 2.5 copy.71
  128.2 2.6 copy.56
  130.8 2.2 copy.75
  134.7 198.7 %while.16 = (s32[]{:T(128)}, bf16[8,1024,128]{1,2,0:T(8,128)(2,1)}, s32[8,64]{1,0:T(8,128)}, s32[8]{0:T(128)S(1)}, bf16[8,1024,128]{2,1,0:T(8,128)(2,1)}, /*inde...) while((s32[]{:T(128)}, bf16[8,1024,128]{1,2,0:T(8,128)(2,1)}, ...), condition=%wide.region_6.7_spmd.clone, body=%wide.region_0.6_spmd.clone.sunk | while | flops 413292544 | bytes 39466960 | solution.py:130
  140.6 2.0 sort.33
  155.8 2.2 fusion.60
  180.6 2.2 fusion.60
  205.4 2.2 fusion.60
  230.3 2.2 fusion.60
  255.1 2.2 fusion.60
  279.9 2.2 fusion.60
  304.8 2.2 fusion.60
  329.6 2.2 fusion.60
  333.4 10.8 %copy.63 = bf16[1,1024,1024]{2,0,1:T(2,128)(2,1)} copy(bf16[1,1024,1024]{1,2,0:T(8,128)(2,1)} %bitcast.122) | data formatting | bytes 4194304 | tf_op jit(solution)/shard_map/reshape | solution.py:140
  344.2 12.8 %reduce.4 = bf16[1024,1024]{1,0:T(8,128)(2,1)S(1)} reduce(bf16[1024,1,1024]{2,1,0:T(2,128)(2,1)} %bitcast.107, bf16[]{:T(256)} %broadcast.358), dimensions={1}, to_apply=%bitcast.65.reduce_sub_computation | reduce | bytes 4194306
  357.1 3.8 reshape.381
  360.8 30.9 %all_to_all.48 = bf16[8,2,65536]{2,1,0:T(2,128)(2,1)S(1)} all-to-all(bf16[8,2,65536]{2,1,0:T(2,128)(2,1)} %reshape.381), channel_id=1, replica_groups=mesh['head'=8,'ctx'=32] {'head'}, dimensions={0} | all-to-all | bytes 4194304 | tf_op jit(solution)/shard_map/all_to_all | solution.py:141
  391.7 4.4 %reshape.382 = bf16[1024,1,1024]{2,1,0:T(2,128)(2,1)} reshape(bf16[8,2,65536]{2,1,0:T(2,128)(2,1)S(1)} %all_to_all.48) | data formatting | bytes 4194304
  396.1 3.0 copy.73
  399.1 2.4 copy.64
  401.5 4.1 copy.65
  (427 shorter events, 168.6 us)
Async XLA Ops:
  6.5 128.2 %all-gather.3.cloned.1.call-start = ((), (), s32[]{:S(2)}) async-start(), calls=%async_computation.3 | async-start | bytes 2162688 | tf_op jit(solution)/shard_map/all_gather | solution.py:51
  12.6 22.2 %copy-start.2 = (bf16[1,128,8192]{2,1,0:T(8,128)(2,1)S(1)}, bf16[1,128,8192]{2,1,0:T(8,128)(2,1)}, u32[]{:S(2)}) copy-start(bf16[1,128,8192]{2,1,0:T(8,128)(2,1)} %param.10) | copy-start | bytes 6291460
  27.6 62.5 %all-to-all-start.1 = ((bf16[8,2,16384]{2,1,0:T(2,128)(2,1)}), bf16[8,2,16384]{2,1,0:T(2,128)(2,1)}, u32[]{:S(2)}, u32[]{:S(2)}) async-start(bf16[8,2,16384]{2,1,0:T(2,128)(2,1)} %reshape.379), calls=%async_computation.1 | async-start | bytes 1048576 | tf_op jit(solution)/shard_map/all_to_all | solution.py:33
  90.1 31.2 %all-to-all-start = ((bf16[8,2,65536]{2,1,0:T(2,128)(2,1)}), bf16[8,2,65536]{2,1,0:T(2,128)(2,1)S(1)}, u32[]{:S(2)}, u32[]{:S(2)}) async-start(bf16[8,2,65536]{2,1,0:T(2,128)(2,1)} %reshape.377), calls=%async_computation | async-start | bytes 4194304 | tf_op jit(solution)/shard_map/all_to_all | solution.py:32
  97.2 4.0 copy-start.4
  101.2 18.4 %collective-permute-start = (bf16[960,1,256]{2,0,1:T(8,128)(2,1)}, bf16[960,1,256]{2,0,1:T(8,128)(2,1)S(1)}, u32[]{:S(2)}, u32[]{:S(2)}) collective-permute-start(bf16[960,1,256]{2,0,1:T(8,128)(2,1)} %slice_select_fusion), channel_id=1, source_target_pairs={{31,0},{0,1},{1,2},{2,3},{3,4},{4,5},{5,6},{6,7},{7,8},{8,9},{9,10... | collective-permute-start | bytes 1474568 | tf_op jit(solution)/shard_map/ppermute | solution.py:16
  133.0 1.7 copy-start.3
  133.0 1.7 copy-start.5
  134.7 4.9 %copy-start.7 = (s32[8]{0:T(128)}, s32[8]{0:T(128)S(1)}, u32[]{:S(2)}) copy-start(s32[8]{0:T(128)S(1)} %get-tuple-element.511) | copy-start | bytes 100 | tf_op jit(solution)/shard_map/while
  154.2 1.6 copy-start
  158.0 1.6 copy-start.6
  159.6 4.9 %copy-start.7 = (s32[8]{0:T(128)}, s32[8]{0:T(128)S(1)}, u32[]{:S(2)}) copy-start(s32[8]{0:T(128)S(1)} %get-tuple-element.511) | copy-start | bytes 100 | tf_op jit(solution)/shard_map/while
  179.0 1.6 copy-start
  182.8 1.6 copy-start.6
  184.4 4.9 %copy-start.7 = (s32[8]{0:T(128)}, s32[8]{0:T(128)S(1)}, u32[]{:S(2)}) copy-start(s32[8]{0:T(128)S(1)} %get-tuple-element.511) | copy-start | bytes 100 | tf_op jit(solution)/shard_map/while
  203.8 1.6 copy-start
  207.7 1.6 copy-start.6
  209.2 4.9 %copy-start.7 = (s32[8]{0:T(128)}, s32[8]{0:T(128)S(1)}, u32[]{:S(2)}) copy-start(s32[8]{0:T(128)S(1)} %get-tuple-element.511) | copy-start | bytes 100 | tf_op jit(solution)/shard_map/while
  228.7 1.6 copy-start
  232.5 1.6 copy-start.6
  234.1 4.9 %copy-start.7 = (s32[8]{0:T(128)}, s32[8]{0:T(128)S(1)}, u32[]{:S(2)}) copy-start(s32[8]{0:T(128)S(1)} %get-tuple-element.511) | copy-start | bytes 100 | tf_op jit(solution)/shard_map/while
  253.5 1.6 copy-start
  257.3 1.6 copy-start.6
  258.9 4.9 %copy-start.7 = (s32[8]{0:T(128)}, s32[8]{0:T(128)S(1)}, u32[]{:S(2)}) copy-start(s32[8]{0:T(128)S(1)} %get-tuple-element.511) | copy-start | bytes 100 | tf_op jit(solution)/shard_map/while
  278.3 1.6 copy-start
  282.2 1.6 copy-start.6
  283.7 4.9 %copy-start.7 = (s32[8]{0:T(128)}, s32[8]{0:T(128)S(1)}, u32[]{:S(2)}) copy-start(s32[8]{0:T(128)S(1)} %get-tuple-element.511) | copy-start | bytes 100 | tf_op jit(solution)/shard_map/while
  303.2 1.6 copy-start
  307.0 1.6 copy-start.6
  308.6 4.9 %copy-start.7 = (s32[8]{0:T(128)}, s32[8]{0:T(128)S(1)}, u32[]{:S(2)}) copy-start(s32[8]{0:T(128)S(1)} %get-tuple-element.511) | copy-start | bytes 100 | tf_op jit(solution)/shard_map/while
  328.0 1.6 copy-start
  331.8 1.6 copy-start.6
  (16 other events, 23.3 us)
Sparse Core Ops, SparseCore 0:
  10.4 77.8 all-gather.2
where the time goes:
time: 416 us; the launch traced here: 412 us
  local copies, waits for them, and re-layouts  140 us (34%)
  other arithmetic  135 us (32%)
  matrix products  40.6 us (10%)
  blocking collectives  30.9 us (7%)
  loops' own time  21.4 us (5%)
  waiting for transfers between devices  18.9 us (5%)
  between operations  13.5 us (3%)
  starting transfers between devices  12.1 us (3%)
    unnamed x3, other arithmetic  70.4 us
    unnamed x24, local copies, waits for them, and re-layouts  40.2 us
    all_to_all x1, blocking collectives, per_device(): lax.all_to_all(outgoing, 'head', split_axis=1, concat_axis=2, tiled=True)  30.9 us
    another operation x1, loops' own time, per_device(): lax.map(one_head, (head_rows, vertical_heads, slash_offsets, slash_counts...  21.4 us
    while x80, local copies, waits for them, and re-layouts  19.8 us
    ppermute x1, waiting for transfers between devices, shifted(): return lax.ppermute(block, axis, route)  18.3 us
    dot_general x8, matrix products, one_head(): jnp.einsum('gqsk,gskd->gqd', slash_weights.astype(jnp.bfloat16), slash_kv...  17.8 us
    dynamic_slice x24, local copies, waits for them, and re-layouts, per_device(): lax.map(one_head, (head_rows, vertical_heads, slash_offsets, slash_counts...  17.3 us
  transfers between devices with their start and end apart: 4, of which 2 were waited for; matrix products, arithmetic and copies ran while one was open for 23% of the time, Pallas kernels for 0%

commit v1 on v0

v1 whole, which is shorter than its diff:
```python
import functools
import math

import jax
import jax.numpy as jnp
from jax import lax
from jax.experimental import pallas as pl
from jax.experimental.pallas import tpu as pltpu
from jax.sharding import PartitionSpec as P

MESH = pl.DeviceIdType.MESH
W = 128
BLK = 64
CH = 128
TAIL = 960
NEG = -1e30
COEF = W**-0.5 * math.log2(math.e)


def kernel(
    ids_ref,
    counts_ref,
    offs_ref,
    slash_ref,
    heads_ref,
    q_ref,
    kv_ref,
    cache_ref,
    out_ref,
    qin,
    obuf,
    band0,
    band1,
    pool0,
    pool1,
    cachev,
    vg,
    par,
    lst,
    lists,
    loc,
    k0s,
    k0r,
    k1s,
    k1r,
    cs,
    qs,
    qr,
    os_,
    or_,
    ts,
    tr,
    xs,
    xr,
    ps,
    pr,
):
    h = lax.axis_index("head")
    c = lax.axis_index("ctx")
    x, core = h // 2, lax.rem(h, 2)
    z, y = c // 4, lax.rem(c, 4)
    far = lax.rem(h + 4, 8)
    D = 1 - 2 * core
    mate = x * 2 + 1 - core
    mate_far = lax.rem(mate + 4, 8)
    nxt = lax.rem(c + 1, 32)
    prv = lax.rem(c + 31, 32)

    def hx(d, cc):
        return hs[d, cc]

    zs = {s: lax.rem(z + s * D + 16, 8) for s in range(-4, 4)}
    ys = {s: lax.rem(y + s * D + 8, 4) for s in range(-2, 3)}
    hs = {(d, cc): lax.rem(x + d + 4, 4) * 2 + cc for d in (-1, 1) for cc in (0, 1)}

    def zz(s):
        return zs[s]

    def yy(s):
        return ys[s]

    def zdev(s):
        return (h, zz(s) * 4 + y)

    def ydev(s):
        return (h, z * 4 + yy(s))

    sent = []
    band, pool = (band0, band1), (pool0, pool1)

    def go(make, cond=None):
        if cond is None:
            make().start()
        else:

            @pl.when(cond())
            def _():
                make().start()

        sent.append((make, cond))

    def remote(src, dst, ss, rs, dev):
        return pltpu.make_async_remote_copy(
            src_ref=src, dst_ref=dst, send_sem=ss, recv_sem=rs, device_id=dev, device_id_type=MESH
        )

    def arrived(dst, ss, rs):
        remote(dst, dst, ss, rs, (h, c)).wait_recv()

    def head_cols(ref, j, width):
        return ref.at[0, :, pl.ds(pl.multiple_of(j * width, width), width)]

    def kv_cols(j):
        return kv_ref.at[:, :, pl.ds(pl.multiple_of(j * 256, 256), 256)]

    def rows_of(s, start, size=CH):
        return band[s].at[pl.ds(start // BLK, size // BLK)]

    load_cache = pltpu.make_async_copy(cache_ref.at[pl.ds(0, 48)], cachev, loc.at[0])
    load_cache.start()
    locals_ = [
        pltpu.make_async_copy(src, dst, loc.at[2 + i])
        for i, (src, dst) in enumerate(
            [
                (kv_cols(h), rows_of(0, TAIL + CH * h)),
                (kv_cols(far), rows_of(1, 1024 + CH * core)),
                (head_cols(q_ref, h, 1024), qin.at[4 + core]),
                (head_cols(q_ref, far, 1024), qin.at[6 + core]),
            ]
        )
    ]
    for cp in locals_:
        cp.start()

    barrier = pltpu.get_barrier_semaphore()

    def greet(dev):
        pl.semaphore_signal(barrier, inc=1, device_id=dev, device_id_type=MESH)

    for s in (-2, -1, 1, 2):
        greet(zdev(s))
    for s in (-1, 1, 2):
        greet(ydev(s))

    @pl.when(c > 0)
    def _():
        for r in range(8):
            greet((r, prv))

    @pl.when(c == 0)
    def _():
        greet((h, 31))
        greet((far, 31))

    for r in range(1, 8):
        greet((lax.rem(h + r, 8), c))

    lane = lax.broadcasted_iota(jnp.int32, (8, 128), 1)
    row = lax.broadcasted_iota(jnp.int32, (8, 128), 0)
    live = jnp.zeros((8, 128), jnp.int32)
    for i in range(32):
        live = jnp.where(lane // 2 == i, counts_ref[0, i], live)
    table = jnp.zeros((8, 128), jnp.int32)
    for j in range(8):
        for i in range(4):
            table = jnp.where((row == j) & (lane == 64 + i), offs_ref[i, j], table)
        table = jnp.where((row == j) & (lane == 68), slash_ref[0, j], table)
    par[0] = table
    par[0, :, 0:64] = jnp.where(lax.rem(lane, 2) < live, 1, 0)[:, 0:64] * heads_ref[...]

    @pl.when(c < 31)
    def _():
        pl.semaphore_wait(barrier, 22)

    @pl.when(c == 31)
    def _():
        pl.semaphore_wait(barrier, 16)

    def piece(k, zpos, ypos):
        return pool[k].at[pl.ds((zpos * 4 + ypos) * 2, 2)]

    load_cache.wait()
    for i in range(2):
        pool0[c * 2 + i] = cachev[ids_ref[0, 0, i]]

    def psend(n, place, to):
        go(lambda: remote(piece(*place()), piece(*place()), ps.at[n], pr.at[n], to()))

    def parrive(n, place):
        arrived(piece(*place()), ps.at[n], pr.at[n])

    Z, YL, YS, YF = 0, 8, 16, 24
    KX, KL, KS, KF, KZ = 32, 33, 34, 35, 36
    zorder = [0, -1, 1, -2, 2, -3, 3, -4]
    yorder = [0, -1, 1, -2]

    def k1_push(n):
        ref = lambda: (0, zz(zorder[n]), y)
        psend(YL + n, ref, lambda: ydev(1))
        psend(YS + n, ref, lambda: ydev(-1))

    def k1_arrive(n):
        ref = lambda: (0, zz(zorder[n]), y)
        parrive(Z + n, ref)
        if n == 3:
            psend(Z + 5, ref, lambda: zdev(1))
            psend(Z + 7, ref, lambda: zdev(2))
        if n == 4:
            psend(Z + 6, ref, lambda: zdev(-1))
        k1_push(n)

    def k1_forward(n):
        ref = lambda: (0, zz(zorder[n]), yy(-1))
        parrive(YL + n, ref)
        psend(YF + n, ref, lambda: ydev(1))

    def k2_zstart(n):
        ref = lambda: (1, z, yy(yorder[n]))
        psend(KZ + n, ref, lambda: zdev(1))
        psend(KZ + 16 + n, ref, lambda: zdev(-1))

    def k2_long(s, n):
        ref = lambda: (1, zz(-s), yy(yorder[n]))
        parrive(KZ + 4 * (s - 1) + n, ref)
        if s < 4:
            psend(KZ + 4 * s + n, ref, lambda: zdev(1))

    def k2_short(s, n):
        ref = lambda: (1, zz(s), yy(yorder[n]))
        parrive(KZ + 16 + 4 * (s - 1) + n, ref)
        if s < 3:
            psend(KZ + 16 + 4 * s + n, ref, lambda: zdev(-1))

    own = lambda: (0, z, y)
    for n, d in ((3, 2), (4, -2), (1, 1), (2, -1)):
        psend(Z + n, own, lambda d=d: zdev(d))
    k1_push(0)

    for r in (4, 2, 3, 5, 6, 1, 7):
        hd = lax.rem(h + r, 8)
        go(
            lambda r=r, hd=hd: remote(
                kv_cols(hd), rows_of(0, TAIL + CH * h), k0s.at[r], k0r.at[h], (hd, c)
            )
        )
    go(lambda: remote(piece(0, z, y), piece(1, z, y), ps.at[KX], pr.at[KX], (far, c)))
    go(lambda: remote(par.at[0], par.at[1], xs.at[0], xr.at[0], (far, c)))

    for d in (1, -1):
        for cc in (0, 1):
            u = (0 if d == 1 else 2) + core
            n = (0 if d == 1 else 2) + cc
            hd = hx(d, cc)
            go(
                lambda u=u, n=n, hd=hd: remote(
                    head_cols(q_ref, hd, 1024), qin.at[u], qs.at[n], qr.at[u], (hd, c)
                )
            )
    go(lambda: remote(head_cols(q_ref, mate, 1024), qin.at[4 + core], qs.at[4], qr.at[4], (mate, c)))
    go(lambda: remote(head_cols(q_ref, mate_far, 1024), qin.at[6 + core], qs.at[5], qr.at[5], (mate, c)))

    for i in range(5):
        xd = lax.rem(x + i, 4)
        cd = lax.rem(c + (x + i) // 4, 32)
        for cc in range(1 if i == 0 else 2):
            hd = mate if i == 0 else xd * 2 + cc
            n = 2 * i + cc
            across = lax.rem(hd + 4, 8)
            go(
                lambda i=i, n=n, hd=hd, cd=cd, across=across: remote(
                    kv_cols(across),
                    rows_of(1, (4 - i) * 256 + CH * core),
                    k1s.at[n],
                    k1r.at[2 * i + core],
                    (hd, cd),
                ),
                None if i == 0 else (lambda i=i: 4 * c + x + i < 128),
            )
    xfar = lax.rem(x + 2, 4)
    for i in range(1, 5):
        back = 64 - 4 * lax.max(i - xfar, 1)
        for cc in range(2):
            go(
                lambda i=i, cc=cc, back=back: remote(
                    cache_ref.at[pl.ds(back + 2 * cc, 2)],
                    rows_of(1, (4 - i) * 256 + CH * cc),
                    cs.at[2 * i + cc],
                    k1r.at[2 * i + cc],
                    (far, 0),
                ),
                lambda i=i: (c == 31) & (i > xfar),
            )

    def make_lists(s):
        rowv = par[s]
        flag = jnp.where(lane < 64, rowv, 0)
        rank = flag
        for step in (1, 2, 4, 8, 16, 32):
            rank = rank + jnp.where(lane >= step, pltpu.roll(rank, step, 1), 0)
        tab = jnp.where(lane >= 64, rowv, 0)
        for i in range(8):
            at = jnp.sum(jnp.where((flag == 1) & (rank == i + 1), lane, 0), axis=1, keepdims=True)
            tab = tab + jnp.where(lane == i, at, 0)
        tab = tab + jnp.where(lane == 8, jnp.sum(flag, axis=1, keepdims=True), 0)
        lst[s] = tab

    make_lists(0)

    @pl.loop(0, 8)
    def _(j):
        vg[j, :, 256:384] = jnp.ones((512, 128), jnp.bfloat16)

    parrive(KX, lambda: (1, z, y))
    psend(KL, lambda: (1, z, y), lambda: ydev(1))
    psend(KS, lambda: (1, z, y), lambda: ydev(-1))
    psend(KF, lambda: (1, z, y), lambda: ydev(2))
    k2_zstart(0)
    k1_arrive(1)
    k1_arrive(2)
    k1_arrive(3)
    k1_arrive(4)
    k1_forward(0)
    arrived(par.at[1], xs.at[0], xr.at[0])
    make_lists(1)
    to_smem = pltpu.make_async_copy(lst, lists, loc.at[1])
    to_smem.start()
    parrive(KL, lambda: (1, z, yy(-1)))
    k2_zstart(1)
    parrive(KS, lambda: (1, z, yy(1)))
    k2_zstart(2)
    parrive(KF, lambda: (1, z, yy(-2)))
    k2_zstart(3)

    for r in range(1, 8):
        src = lax.rem(h + r, 8)
        arrived(rows_of(0, TAIL + CH * src), k0s.at[r], k0r.at[src])
    locals_[0].wait()
    go(
        lambda: remote(rows_of(0, TAIL + BLK, TAIL), rows_of(0, 0, TAIL), ts.at[0], tr.at[0], (h, nxt)),
        lambda: c != 31,
    )
    go(
        lambda: remote(
            cache_ref.at[pl.ds(49, 15)], rows_of(0, 0, TAIL), ts.at[0], tr.at[0], (h, nxt)
        ),
        lambda: c == 31,
    )

    k2_long(1, 0)
    k2_short(1, 0)
    k1_forward(1)
    k1_forward(2)
    k1_arrive(5)
    k1_arrive(6)
    k1_arrive(7)
    k1_forward(3)
    k1_forward(4)
    for n in range(1, 4):
        k2_long(1, n)
        k2_short(1, n)
    k1_forward(5)
    k1_forward(6)
    k1_forward(7)
    for n in range(4):
        k2_long(2, n)
        k2_short(2, n)
    for n in range(8):
        parrive(YS + n, lambda n=n: (0, zz(zorder[n]), yy(1)))
    for n in range(8):
        parrive(YF + n, lambda n=n: (0, zz(zorder[n]), yy(-2)))
    to_smem.wait()
    arrived(rows_of(0, 0, TAIL), ts.at[0], tr.at[0])

    def gather(s):
        @pl.loop(0, 8)
        def _(j):
            for i in range(8):
                vg[j, pl.ds(i * BLK, BLK), 0:256] = pool[s][jnp.clip(lists[s, j, i], 0, 63)]

    nt = (((1,), (1,)), ((), ()))
    f32, bf = jnp.float32, jnp.bfloat16

    def attend(p, s, first, j):
        cols = slice(j * W, (j + 1) * W)
        q = jnp.concatenate([qin[2 * p, :, cols], qin[2 * p + 1, :, cols]], axis=0)
        vlane = lax.broadcasted_iota(jnp.int32, (1, 512), 1)
        vbias = jnp.where(vlane < lists[s, j, 8] * BLK, 0.0, NEG)
        qrow = lax.broadcasted_iota(jnp.int32, (BLK, 256), 0)
        krow = lax.broadcasted_iota(jnp.int32, (BLK, 256), 1)
        keep = ((krow >= BLK) | (krow <= qrow)) & (krow < lists[s, j, 68] * BLK)
        sv = lax.dot_general(q, vg[j, :, :W], nt, preferred_element_type=f32)
        pvs, accs = [], []
        for b in range(4):
            keys = []
            for i in range(4):
                start = first + b
                if i:
                    start = start - jnp.clip(lists[s, j, 64 + i], 0, 15)
                keys.append(band[s][start])
            ks = jnp.concatenate(keys, axis=0)
            part = slice(b * BLK, (b + 1) * BLK)
            ss = lax.dot_general(q[part], ks[:, :W], nt, preferred_element_type=f32)
            tv = sv[part] * COEF + vbias
            tsl = jnp.where(keep, ss * COEF, NEG)
            m = jnp.maximum(jnp.max(tv, axis=1, keepdims=True), jnp.max(tsl, axis=1, keepdims=True))
            pvs.append(jnp.exp2(tv - m).astype(bf))
            psl = jnp.exp2(tsl - m).astype(bf)
            vs = jnp.concatenate([ks[:, W:], jnp.ones((256, W), bf)], axis=1)
            accs.append(jnp.dot(psl, vs, preferred_element_type=f32))
        acc = jnp.dot(jnp.concatenate(pvs, axis=0), vg[j, :, W:], preferred_element_type=f32)
        acc += jnp.concatenate(accs, axis=0)
        o = (acc[:, :W] / acc[:, W:]).astype(bf)
        obuf[2 * p, :, cols] = o[:CH]
        obuf[2 * p + 1, :, cols] = o[CH:]

    def out_remote(p, cc):
        d = -1 if p == 0 else 1
        return lambda: remote(
            obuf.at[2 * p + cc],
            head_cols(out_ref, h, 1024),
            os_.at[2 * p + cc],
            or_.at[(2 if d == -1 else 0) + core],
            (hx(d, cc), c),
        )

    def out_mate(p):
        return lambda: remote(
            obuf.at[2 * p + 1 - core],
            head_cols(out_ref, h if p == 2 else far, 1024),
            os_.at[2 + p],
            or_.at[2 + p],
            (mate, c),
        )

    def own_out(p):
        return pltpu.make_async_copy(
            obuf.at[2 * p + core], head_cols(out_ref, h if p == 2 else far, 1024), loc.at[p]
        )

    gather(0)
    before, after = lax.rem(x + 3, 4), lax.rem(x + 1, 4)

    @pl.loop(0, 3)
    def _(p):
        for d in range(2):

            @pl.when(p == d)
            def _(d=d):
                for u in (2 * d, 2 * d + 1):
                    arrived(qin.at[u], qs.at[u], qr.at[u])

        @pl.when(p == 2)
        def _():
            arrived(qin.at[4 + 1 - core], qs.at[4], qr.at[4])
            locals_[2].wait()

        first = 15 + 4 * jnp.where(p == 0, before, jnp.where(p == 1, after, x))
        for j in range(8):
            attend(p, 0, first, j)

        for d in range(2):

            @pl.when(p == d)
            def _(d=d):
                out_remote(d, 0)().start()
                out_remote(d, 1)().start()
                for n in (2 * d, 2 * d + 1):
                    k2_long(3, n)
                    k2_short(3, n)

        @pl.when(p == 2)
        def _():
            out_mate(2)().start()
            own_out(2).start()

    for n in range(4):
        k2_long(4, n)
    for i in range(1, 5):
        for cc in range(2):
            arrived(rows_of(1, (4 - i) * 256 + CH * cc), k1s.at[2 * i + cc], k1r.at[2 * i + cc])
    arrived(rows_of(1, 1024 + CH * (1 - core)), k1s.at[0], k1r.at[1 - core])
    locals_[1].wait()
    gather(1)
    arrived(qin.at[6 + 1 - core], qs.at[5], qr.at[5])
    locals_[3].wait()
    for j in range(8):
        attend(3, 1, 16, j)
    out_mate(3)().start()
    own_out(3).start()

    for d in (2, 3):
        own_out(d).wait()
    for n in range(4):
        k = hx(1 if n >= 2 else -1, n % 2)
        arrived(head_cols(out_ref, k, 1024), os_.at[n], or_.at[n])
    arrived(head_cols(out_ref, mate, 1024), os_.at[4], or_.at[4])
    arrived(head_cols(out_ref, mate_far, 1024), os_.at[5], or_.at[5])
    for make in (out_remote(0, 0), out_remote(0, 1), out_remote(1, 0), out_remote(1, 1), out_mate(2), out_mate(3)):
        make().wait_send()
    for make, cond in sent:
        if cond is None:
            make().wait_send()
        else:

            @pl.when(cond())
            def _(make=make):
                make().wait_send()


def finish(src, dst, sems):
    copies = [
        pltpu.make_async_copy(src.at[0, pl.ds(16 * i, 16)], dst.at[0, pl.ds(16 * i, 16)], sems.at[i])
        for i in range(8)
    ]
    for cp in copies:
        cp.start()
    for cp in copies:
        cp.wait()


def per_device(
    queries,
    segment_kv,
    cache_kv,
    vertical_ids,
    vertical_counts,
    vertical_heads,
    slash_offsets,
    slash_counts,
):
    bf = jnp.bfloat16
    dma = pltpu.SemaphoreType.DMA
    hbm = pl.BlockSpec(memory_space=pltpu.HBM)
    smem = pl.BlockSpec(memory_space=pltpu.SMEM)
    vmem = pl.BlockSpec(memory_space=pltpu.VMEM)
    shape = jax.ShapeDtypeStruct((1, CH, 8192), bf)
    result = pl.pallas_call(
        kernel,
        out_shape=shape,
        in_specs=[smem, smem, smem, smem, vmem, hbm, hbm, hbm],
        out_specs=vmem,
        scratch_shapes=[
            pltpu.VMEM((8, CH, 1024), bf),
            pltpu.VMEM((8, CH, 1024), bf),
            pltpu.VMEM((31, BLK, 256), bf),
            pltpu.VMEM((20, BLK, 256), bf),
            pltpu.VMEM((64, BLK, 256), bf),
            pltpu.VMEM((64, BLK, 256), bf),
            pltpu.VMEM((48, BLK, 256), bf),
            pltpu.VMEM((8, 512, 384), bf),
            pltpu.VMEM((2, 8, 128), jnp.int32),
            pltpu.VMEM((2, 8, 128), jnp.int32),
            pltpu.SMEM((2, 8, 128), jnp.int32),
            dma((6,)),
            dma((8,)),
            dma((8,)),
            dma((10,)),
            dma((10,)),
            dma((10,)),
            dma((6,)),
            dma((6,)),
            dma((6,)),
            dma((6,)),
            dma((1,)),
            dma((1,)),
            dma((1,)),
            dma((1,)),
            dma((64,)),
            dma((64,)),
        ],
        compiler_params=pltpu.CompilerParams(
            collective_id=0, has_side_effects=True, vmem_limit_bytes=60 << 20
        ),
        cost_estimate=pl.CostEstimate(
            flops=2 * 2 * 8 * 1024 * 768 * W, bytes_accessed=8 << 20, transcendentals=8 * 1024 * 768
        ),
    )(
        vertical_ids,
        vertical_counts,
        slash_offsets.T,
        slash_counts.reshape(1, 8),
        vertical_heads,
        queries,
        segment_kv.reshape(2, BLK, 2048),
        cache_kv.reshape(64, BLK, 256),
    )
    return pl.pallas_call(
        finish,
        out_shape=shape,
        in_specs=[pl.BlockSpec(memory_space=pl.ANY)],
        out_specs=hbm,
        scratch_shapes=[dma((8,))],
        compiler_params=pltpu.CompilerParams(vmem_limit_bytes=8 << 20),
    )(result)


def solution(mesh):
    in_specs = (
        P("ctx", "head", None),
        P("ctx", "head", None),
        P("ctx", "head"),
        P("head", "ctx", None),
        P("head", None),
        P("head", None),
        P("head", None),
        P("head"),
    )
    return jax.shard_map(
        per_device,
        mesh=mesh,
        in_specs=in_specs,
        out_specs=P("ctx", "head", None),
        check_vma=False,
    )
```

time: 416 us -> 83.5 us (0.20)
  local copies, waits for them, and re-layouts: 140 us -> 1.58 us
  other arithmetic: 135 us -> 0 us
  Pallas kernels: 0 us -> 81.8 us
  matrix products: 40.6 us -> 0 us
  blocking collectives: 30.9 us -> 0 us
  loops' own time: 21.4 us -> 0 us
  waiting for transfers between devices: 18.9 us -> 0 us
  between operations: 13.5 us -> 0.02 us
  starting transfers between devices: 12.1 us -> 0 us
    pallas_call x0 -> x2, Pallas kernels: none -> 81.8 us  [the longest x1 80.4 us: per_device(): pl.pallas_call(kernel, out_shape=shape, in_specs=[smem, smem, smem, smem,...]
    unnamed x3 -> x0, other arithmetic: 70.4 us -> none
    dot_general x32 -> x0, matrix products: 40.6 us -> none  [the longest x8 17.8 us: one_head(): jnp.einsum('gqsk,gskd->gqd', slash_weights.astype(jnp.bfloat16), slash_kv...]
    unnamed x24 -> x2, local copies, waits for them, and re-layouts: 40.2 us -> 1.58 us
    select_n x42 -> x0, other arithmetic: 33.4 us -> none  [the longest x8 14.2 us: one_head(): head_pool = jnp.take(pool_blocks, kv_pick, axis=0)]
    all_to_all x1 -> x0, blocking collectives: 30.9 us -> none  [per_device(): lax.all_to_all(outgoing, 'head', split_axis=1, concat_axis=2, tiled=True)]
    gather x25 -> x0, local copies, waits for them, and re-layouts: 28.2 us -> none  [the longest x8 15.8 us: one_head(): slash_kv = head_band[band_index]]
    another operation x1 -> x0, loops' own time: 21.4 us -> none  [per_device(): lax.map(one_head, (head_rows, vertical_heads, slash_offsets, slash_counts...]
  transfers between devices with their start and end apart: 4 -> 0, of which waited for: 2 -> 0; matrix products, arithmetic and copies ran while one was open for 23% -> 0% of each run, Pallas kernels for 0% -> 0%
where the time goes in v1:
time: 83.5 us; the launch traced here: 83.4 us
  Pallas kernels  81.8 us (98%)
  local copies, waits for them, and re-layouts  1.58 us (2%)
    pallas_call x1, Pallas kernels, per_device(): pl.pallas_call(kernel, out_shape=shape, in_specs=[smem, smem, smem, smem,...  80.4 us

profile of v1, /device:TPU:1, one launch (start us, length us, event | category | flops | bytes accessed | tf_op | source)
XLA Modules:
  0.0 83.4 jit_solution(1199166805287635442)
XLA Ops:
  0.0 80.4 %shard_map.82.src = bf16[1,128,8192]{2,1,0:T(8,128)(2,1)} custom-call(s32[1,1,2]{2,1,0:T(1,128)} %ids_ref.1, s32[1,32]{1,0:T(1,128)} %counts_ref.1, s32[4,8]{1,0:T(4,128)} %bitcast.6, s32[1,8]{1,0:T(1,128)} %bitcast.7, s32[8,64]{1,0:T(8,128)} %heads_ref.1, bf16[1,128,8192]{2,1,0:T(8,128)(2,1)} %q_ref.1, bf16[2,64,2048]{2,1,0:T(8,128)(2,1)} %bitcast.5, ...), custom_call_target="tpu_custom_call" | custom-call | flops 3221225472 | bytes 8388608 | tf_op jit(solution)/shard_map/pallas_call | solution.py:537
  80.4 0.0 copy-start
  80.4 1.6 %copy-done = bf16[1,128,8192]{2,1,0:T(8,128)(2,1)S(1)} copy-done((bf16[1,128,8192]{2,1,0:T(8,128)(2,1)S(1)}, bf16[1,128,8192]{2,1,0:T(8,128)(2,1)}, u32[]{:S(2)}) %copy-start) | copy-done | bytes 2097176
  82.0 1.4 %shard_map.83 = bf16[1,128,8192]{2,1,0:T(8,128)(2,1)} custom-call(bf16[1,128,8192]{2,1,0:T(8,128)(2,1)S(1)} %copy-done), custom_call_target="tpu_custom_call" | custom-call | tf_op jit(solution)/shard_map/pallas_call | solution.py:587
Async XLA Ops:
  80.4 1.6 %copy-start = (bf16[1,128,8192]{2,1,0:T(8,128)(2,1)S(1)}, bf16[1,128,8192]{2,1,0:T(8,128)(2,1)}, u32[]{:S(2)}) copy-start(bf16[1,128,8192]{2,1,0:T(8,128)(2,1)} %shard_map.82.src) | copy-start | bytes 6291460

commit v2 on v1

v2 whole, which is shorter than its diff:
```python
import functools
import math

import jax
import jax.numpy as jnp
from jax import lax
from jax.experimental import pallas as pl
from jax.experimental.pallas import tpu as pltpu
from jax.sharding import PartitionSpec as P

MESH = pl.DeviceIdType.MESH
W = 128
BLK = 64
CH = 128
TAIL = 960
NEG = -1e30
ORDER = (2, 1, 3)
COEF = W**-0.5 * math.log2(math.e)


def kernel(
    ids_ref,
    counts_ref,
    offs_ref,
    slash_ref,
    heads_ref,
    q_ref,
    kv_ref,
    cache_ref,
    out_ref,
    qin,
    obuf,
    band0,
    pool0,
    cachev,
    vg,
    par,
    lst,
    lists,
    loc,
    k0s,
    k0r,
    qs,
    qr,
    os_,
    or_,
    ts,
    tr,
    ps,
    pr,
):
    h = lax.axis_index("head")
    c = lax.axis_index("ctx")
    x, core = h // 2, lax.rem(h, 2)
    z, y = c // 4, lax.rem(c, 4)
    D = -1
    nxt = lax.rem(c + 1, 32)
    prv = lax.rem(c + 31, 32)

    zs = {s: lax.rem(z + s * D + 16, 8) for s in range(-4, 4)}
    ys = {s: lax.rem(y + s * D + 8, 4) for s in range(-2, 3)}
    def zz(s):
        return zs[s]

    def yy(s):
        return ys[s]

    def zdev(s):
        return (h, zz(s) * 4 + y)

    def ydev(s):
        return (h, z * 4 + yy(s))

    sent = []

    def go(make, cond=None):
        if cond is None:
            make().start()
        else:

            @pl.when(cond())
            def _():
                make().start()

        sent.append((make, cond))

    def remote(src, dst, ss, rs, dev):
        return pltpu.make_async_remote_copy(
            src_ref=src, dst_ref=dst, send_sem=ss, recv_sem=rs, device_id=dev, device_id_type=MESH
        )

    def arrived(dst, ss, rs):
        remote(dst, dst, ss, rs, (h, c)).wait_recv()

    def head_cols(ref, j, width):
        return ref.at[0, :, pl.ds(pl.multiple_of(j * width, width), width)]

    def kv_cols(j):
        return kv_ref.at[:, :, pl.ds(pl.multiple_of(j * 256, 256), 256)]

    def rows_of(start, size=CH):
        return band0.at[pl.ds(start // BLK, size // BLK)]

    load_cache = pltpu.make_async_copy(cache_ref.at[pl.ds(0, 48)], cachev, loc.at[0])
    load_cache.start()
    locals_ = [
        pltpu.make_async_copy(src, dst, loc.at[2 + i])
        for i, (src, dst) in enumerate(
            [
                (kv_cols(h), rows_of(TAIL + CH * h)),
                (head_cols(q_ref, h, 1024), qin.at[h]),
            ]
        )
    ]
    for cp in locals_:
        cp.start()

    barrier = pltpu.get_barrier_semaphore()

    def greet(dev):
        pl.semaphore_signal(barrier, inc=1, device_id=dev, device_id_type=MESH)

    for s in (-2, -1, 1, 2):
        greet(zdev(s))
    for s in (-1, 1):
        greet(ydev(s))

    greet((h, prv))
    for r in range(1, 8):
        greet((lax.rem(h + r, 8), c))

    lane = lax.broadcasted_iota(jnp.int32, (8, 128), 1)
    row = lax.broadcasted_iota(jnp.int32, (8, 128), 0)
    live = jnp.zeros((8, 128), jnp.int32)
    for i in range(32):
        live = jnp.where(lane // 2 == i, counts_ref[0, i], live)
    table = jnp.zeros((8, 128), jnp.int32)
    for j in range(8):
        for i in range(4):
            table = jnp.where((row == j) & (lane == 64 + i), offs_ref[i, j], table)
        table = jnp.where((row == j) & (lane == 68), slash_ref[0, j], table)
    par[0] = table
    par[0, :, 0:64] = jnp.where(lax.rem(lane, 2) < live, 1, 0)[:, 0:64] * heads_ref[...]

    pl.semaphore_wait(barrier, 14)

    def piece(k, zpos, ypos):
        return pool0.at[pl.ds((zpos * 4 + ypos) * 2, 2)]

    load_cache.wait()
    for i in range(2):
        pool0[c * 2 + i] = cachev[ids_ref[0, 0, i]]

    def psend(n, place, to):
        go(lambda: remote(piece(*place()), piece(*place()), ps.at[n], pr.at[n], to()))

    def parrive(n, place):
        arrived(piece(*place()), ps.at[n], pr.at[n])

    Z, YL, YS, YF = 0, 8, 16, 24
    zorder = [0, -1, 1, -2, 2, -3, 3, -4]

    def k1_push(n):
        ref = lambda: (0, zz(zorder[n]), y)
        psend(YL + n, ref, lambda: ydev(1))
        psend(YS + n, ref, lambda: ydev(-1))

    def k1_arrive(n):
        ref = lambda: (0, zz(zorder[n]), y)
        parrive(Z + n, ref)
        if n == 3:
            psend(Z + 5, ref, lambda: zdev(1))
            psend(Z + 7, ref, lambda: zdev(2))
        if n == 4:
            psend(Z + 6, ref, lambda: zdev(-1))
        k1_push(n)

    def k1_forward(n):
        ref = lambda: (0, zz(zorder[n]), yy(-1))
        parrive(YL + n, ref)
        psend(YF + n, ref, lambda: ydev(1))

    own = lambda: (0, z, y)
    for n, d in ((3, 2), (4, -2), (1, 1), (2, -1)):
        psend(Z + n, own, lambda d=d: zdev(d))
    k1_push(0)

    for r in (4, 2, 3, 5, 6, 1, 7):
        hd = lax.rem(h + r, 8)
        go(
            lambda r=r, hd=hd: remote(
                kv_cols(hd), rows_of(TAIL + CH * h), k0s.at[r], k0r.at[h], (hd, c)
            )
        )
    row_h = [lax.rem(x * 2 + r, 8) for r in range(8)]

    def send_q(n, hd):
        go(lambda: remote(head_cols(q_ref, hd, 1024), qin.at[h], qs.at[n], qr.at[h], (hd, c)))

    send_q(4, row_h[4])
    send_q(5, row_h[5])

    def make_lists(s):
        rowv = par[s]
        flag = jnp.where(lane < 64, rowv, 0)
        rank = flag
        for step in (1, 2, 4, 8, 16, 32):
            rank = rank + jnp.where(lane >= step, pltpu.roll(rank, step, 1), 0)
        tab = jnp.where(lane >= 64, rowv, 0)
        for i in range(8):
            at = jnp.sum(jnp.where((flag == 1) & (rank == i + 1), lane, 0), axis=1, keepdims=True)
            tab = tab + jnp.where(lane == i, at, 0)
        tab = tab + jnp.where(lane == 8, jnp.sum(flag, axis=1, keepdims=True), 0)
        lst[s] = tab

    make_lists(0)

    @pl.loop(0, 8)
    def _(j):
        vg[j, :, 256:384] = jnp.ones((512, 128), jnp.bfloat16)

    k1_arrive(1)
    k1_arrive(2)
    k1_arrive(3)
    k1_arrive(4)
    k1_forward(0)
    to_smem = pltpu.make_async_copy(lst, lists, loc.at[1])
    to_smem.start()
    for r in range(1, 8):
        src = lax.rem(h + r, 8)
        arrived(rows_of(TAIL + CH * src), k0s.at[r], k0r.at[src])
    locals_[0].wait()
    go(
        lambda: remote(rows_of(TAIL + BLK, TAIL), rows_of(0, TAIL), ts.at[0], tr.at[0], (h, nxt)),
        lambda: c != 31,
    )
    go(
        lambda: remote(
            cache_ref.at[pl.ds(49, 15)], rows_of(0, TAIL), ts.at[0], tr.at[0], (h, nxt)
        ),
        lambda: c == 31,
    )

    for n in (2, 6, 3, 7):
        send_q(n, row_h[n])
    send_q(1, x * 2 + 1 - core)
    k1_forward(1)
    k1_forward(2)
    k1_arrive(5)
    k1_arrive(6)
    k1_arrive(7)
    k1_forward(3)
    k1_forward(4)
    k1_forward(5)
    k1_forward(6)
    k1_forward(7)
    for n in range(8):
        parrive(YS + n, lambda n=n: (0, zz(zorder[n]), yy(1)))
    for n in range(8):
        parrive(YF + n, lambda n=n: (0, zz(zorder[n]), yy(-2)))
    to_smem.wait()
    arrived(rows_of(0, TAIL), ts.at[0], tr.at[0])

    def gather(s):
        @pl.loop(0, 8)
        def _(j):
            for i in range(8):
                vg[j, pl.ds(i * BLK, BLK), 0:256] = pool0[jnp.clip(lists[s, j, i], 0, 63)]

    nt = (((1,), (1,)), ((), ()))
    f32, bf = jnp.float32, jnp.bfloat16

    def attend(p, s, first, j):
        cols = slice(j * W, (j + 1) * W)
        q = jnp.concatenate([qin[2 * p, :, cols], qin[2 * p + 1, :, cols]], axis=0)
        vlane = lax.broadcasted_iota(jnp.int32, (1, 512), 1)
        vbias = jnp.where(vlane < lists[s, j, 8] * BLK, 0.0, NEG)
        qrow = lax.broadcasted_iota(jnp.int32, (BLK, 256), 0)
        krow = lax.broadcasted_iota(jnp.int32, (BLK, 256), 1)
        keep = ((krow >= BLK) | (krow <= qrow)) & (krow < lists[s, j, 68] * BLK)
        sv = lax.dot_general(q, vg[j, :, :W], nt, preferred_element_type=f32)
        pvs, accs = [], []
        for b in range(4):
            keys = []
            for i in range(4):
                start = first + b
                if i:
                    start = start - jnp.clip(lists[s, j, 64 + i], 0, 15)
                keys.append(band0[start])
            ks = jnp.concatenate(keys, axis=0)
            part = slice(b * BLK, (b + 1) * BLK)
            ss = lax.dot_general(q[part], ks[:, :W], nt, preferred_element_type=f32)
            tv = sv[part] * COEF + vbias
            tsl = jnp.where(keep, ss * COEF, NEG)
            m = jnp.maximum(jnp.max(tv, axis=1, keepdims=True), jnp.max(tsl, axis=1, keepdims=True))
            pvs.append(jnp.exp2(tv - m).astype(bf))
            psl = jnp.exp2(tsl - m).astype(bf)
            vs = jnp.concatenate([ks[:, W:], jnp.ones((256, W), bf)], axis=1)
            accs.append(jnp.dot(psl, vs, preferred_element_type=f32))
        acc = jnp.dot(jnp.concatenate(pvs, axis=0), vg[j, :, W:], preferred_element_type=f32)
        acc += jnp.concatenate(accs, axis=0)
        o = (acc[:, :W] / acc[:, W:]).astype(bf)
        obuf[2 * p, :, cols] = o[:CH]
        obuf[2 * p + 1, :, cols] = o[CH:]

    def out_copy(dev, n, to, half):
        return remote(
            obuf.at[dev, :, 512 * half : 512 * half + 512],
            head_cols(out_ref, 2 * h + half, 512),
            os_.at[2 * n + half],
            or_.at[2 * h + half],
            (to, c),
        )

    own_out = pltpu.make_async_copy(obuf.at[h], head_cols(out_ref, h, 1024), loc.at[2])
    gather(0)
    chips = [lax.rem(x + r, 4) for r in range(4)]

    @pl.loop(0, 4)
    def _(t):
        for r in range(1, 4):

            @pl.when(t == ORDER.index(r))
            def _(r=r):
                for cc in range(2):
                    src = row_h[2 * r + cc]
                    arrived(qin.at[src], qs.at[1], qr.at[src])

        @pl.when(t == 3)
        def _():
            other = x * 2 + 1 - core
            arrived(qin.at[other], qs.at[1], qr.at[other])
            locals_[1].wait()

        p = jnp.where(t == 0, chips[ORDER[0]], jnp.where(t == 1, chips[ORDER[1]], jnp.where(t == 2, chips[ORDER[2]], x)))
        for half in range(2):
            for j in range(4 * half, 4 * half + 4):
                attend(p, 0, 15 + 4 * p, j)

            for r in range(1, 4):

                @pl.when(t == ORDER.index(r))
                def _(r=r, half=half):
                    for cc in range(2):
                        to = row_h[2 * r + cc]
                        out_copy(to, 2 * r + cc, to, half).start()

    other = x * 2 + 1 - core
    for half in range(2):
        out_copy(other, 1, other, half).start()
    own_out.start()
    own_out.wait()
    for r in range(1, 8):
        k = lax.rem(h + r, 8)
        for half in range(2):
            arrived(head_cols(out_ref, 2 * k + half, 512), os_.at[1], or_.at[2 * k + half])
    for half in range(2):
        for r in range(2, 8):
            out_copy(row_h[r], r, row_h[r], half).wait_send()
        out_copy(other, 1, other, half).wait_send()
    for make, cond in sent:
        if cond is None:
            make().wait_send()
        else:

            @pl.when(cond())
            def _(make=make):
                make().wait_send()


def finish(src, dst, sems):
    copies = [
        pltpu.make_async_copy(src.at[0, pl.ds(16 * i, 16)], dst.at[0, pl.ds(16 * i, 16)], sems.at[i])
        for i in range(8)
    ]
    for cp in copies:
        cp.start()
    for cp in copies:
        cp.wait()


def per_device(
    queries,
    segment_kv,
    cache_kv,
    vertical_ids,
    vertical_counts,
    vertical_heads,
    slash_offsets,
    slash_counts,
):
    bf = jnp.bfloat16
    dma = pltpu.SemaphoreType.DMA
    hbm = pl.BlockSpec(memory_space=pltpu.HBM)
    smem = pl.BlockSpec(memory_space=pltpu.SMEM)
    vmem = pl.BlockSpec(memory_space=pltpu.VMEM)
    shape = jax.ShapeDtypeStruct((1, CH, 8192), bf)
    result = pl.pallas_call(
        kernel,
        out_shape=shape,
        in_specs=[smem, smem, smem, smem, vmem, hbm, hbm, hbm],
        out_specs=vmem,
        scratch_shapes=[
            pltpu.VMEM((8, CH, 1024), bf),
            pltpu.VMEM((8, CH, 1024), bf),
            pltpu.VMEM((31, BLK, 256), bf),
            pltpu.VMEM((64, BLK, 256), bf),
            pltpu.VMEM((48, BLK, 256), bf),
            pltpu.VMEM((8, 512, 384), bf),
            pltpu.VMEM((1, 8, 128), jnp.int32),
            pltpu.VMEM((1, 8, 128), jnp.int32),
            pltpu.SMEM((1, 8, 128), jnp.int32),
            dma((6,)),
            dma((8,)),
            dma((8,)),
            dma((8,)),
            dma((8,)),
            dma((16,)),
            dma((16,)),
            dma((1,)),
            dma((1,)),
            dma((32,)),
            dma((32,)),
        ],
        compiler_params=pltpu.CompilerParams(
            collective_id=0, has_side_effects=True, vmem_limit_bytes=60 << 20
        ),
        cost_estimate=pl.CostEstimate(
            flops=2 * 2 * 8 * 1024 * 768 * W, bytes_accessed=8 << 20, transcendentals=8 * 1024 * 768
        ),
    )(
        vertical_ids,
        vertical_counts,
        slash_offsets.T,
        slash_counts.reshape(1, 8),
        vertical_heads,
        queries,
        segment_kv.reshape(2, BLK, 2048),
        cache_kv.reshape(64, BLK, 256),
    )
    return pl.pallas_call(
        finish,
        out_shape=shape,
        in_specs=[pl.BlockSpec(memory_space=pl.ANY)],
        out_specs=hbm,
        scratch_shapes=[dma((8,))],
        compiler_params=pltpu.CompilerParams(vmem_limit_bytes=8 << 20),
    )(result)


def solution(mesh):
    in_specs = (
        P("ctx", "head", None),
        P("ctx", "head", None),
        P("ctx", "head"),
        P("head", "ctx", None),
        P("head", None),
        P("head", None),
        P("head", None),
        P("head"),
    )
    return jax.shard_map(
        per_device,
        mesh=mesh,
        in_specs=in_specs,
        out_specs=P("ctx", "head", None),
        check_vma=False,
    )
```

time: 83.5 us -> 70.4 us (0.84)
  Pallas kernels: 81.8 us -> 68.6 us
    pallas_call x1, Pallas kernels: 80.4 us -> 67.2 us  [per_device(): pl.pallas_call(kernel, out_shape=shape, in_specs=[smem, smem, smem, smem,...]
where the time goes in v2:
time: 70.4 us; the launch traced here: 70.2 us
  Pallas kernels  68.6 us (97%)
  local copies, waits for them, and re-layouts  1.58 us (2%)
    pallas_call x1, Pallas kernels, per_device(): pl.pallas_call(kernel, out_shape=shape, in_specs=[smem, smem, smem, smem,...  67.2 us
    unnamed x2, local copies, waits for them, and re-layouts  1.58 us

profile of v2, /device:TPU:1, one launch (start us, length us, event | category | flops | bytes accessed | tf_op | source)
XLA Modules:
  0.0 70.2 jit_solution(15362630344110378894)
XLA Ops:
  0.0 67.2 %shard_map.82.src = bf16[1,128,8192]{2,1,0:T(8,128)(2,1)} custom-call(s32[1,1,2]{2,1,0:T(1,128)} %ids_ref.1, s32[1,32]{1,0:T(1,128)} %counts_ref.1, s32[4,8]{1,0:T(4,128)} %bitcast.6, s32[1,8]{1,0:T(1,128)} %bitcast.7, s32[8,64]{1,0:T(8,128)} %heads_ref.1, bf16[1,128,8192]{2,1,0:T(8,128)(2,1)} %q_ref.1, bf16[2,64,2048]{2,1,0:T(8,128)(2,1)} %bitcast.5, ...), custom_call_target="tpu_custom_call" | custom-call | flops 3221225472 | bytes 8388608 | tf_op jit(solution)/shard_map/pallas_call | solution.py:398
  67.3 0.0 copy-start
  67.3 1.6 %copy-done = bf16[1,128,8192]{2,1,0:T(8,128)(2,1)S(1)} copy-done((bf16[1,128,8192]{2,1,0:T(8,128)(2,1)S(1)}, bf16[1,128,8192]{2,1,0:T(8,128)(2,1)}, u32[]{:S(2)}) %copy-start) | copy-done | bytes 2097176
  68.8 1.4 %shard_map.83 = bf16[1,128,8192]{2,1,0:T(8,128)(2,1)} custom-call(bf16[1,128,8192]{2,1,0:T(8,128)(2,1)S(1)} %copy-done), custom_call_target="tpu_custom_call" | custom-call | tf_op jit(solution)/shard_map/pallas_call | solution.py:441
Async XLA Ops:
  67.3 1.6 %copy-start = (bf16[1,128,8192]{2,1,0:T(8,128)(2,1)S(1)}, bf16[1,128,8192]{2,1,0:T(8,128)(2,1)}, u32[]{:S(2)}) copy-start(bf16[1,128,8192]{2,1,0:T(8,128)(2,1)} %shard_map.82.src) | copy-start | bytes 6291460

commit v3 on v2

--- a/solution.py
+++ b/solution.py
@@ -145,7 +145,7 @@
     pl.semaphore_wait(barrier, 14)
 
     def piece(k, zpos, ypos):
-        return pool0.at[pl.ds((zpos * 4 + ypos) * 2, 2)]
+        return pool0.at[pl.ds((zpos * 4 + ypos) * 2 + k, 1)]
 
     load_cache.wait()
     for i in range(2):
@@ -180,7 +180,27 @@
         parrive(YL + n, ref)
         psend(YF + n, ref, lambda: ydev(1))
 
+    BY, BZ = 32, 34
+    yorder = [0, -1, 1, -2]
+
+    def b_start(i):
+        ref = lambda: (1, z, yy(yorder[i]))
+        for m, d in ((3, 2), (4, -2), (1, 1), (2, -1)):
+            psend(BZ + 7 * i + m, ref, lambda d=d: zdev(d))
+
+    def b_arrive(i, m):
+        ref = lambda: (1, zz(zorder[m]), yy(yorder[i]))
+        parrive(BZ + 7 * i + m, ref)
+        if m == 3:
+            psend(BZ + 7 * i + 5, ref, lambda: zdev(1))
+            psend(BZ + 7 * i + 7, ref, lambda: zdev(2))
+        if m == 4:
+            psend(BZ + 7 * i + 6, ref, lambda: zdev(-1))
+
     own = lambda: (0, z, y)
+    psend(BY, lambda: (1, z, y), lambda: ydev(1))
+    psend(BY + 1, lambda: (1, z, y), lambda: ydev(-1))
+    b_start(0)
     for n, d in ((3, 2), (4, -2), (1, 1), (2, -1)):
         psend(Z + n, own, lambda d=d: zdev(d))
     k1_push(0)
@@ -219,6 +239,11 @@
     def _(j):
         vg[j, :, 256:384] = jnp.ones((512, 128), jnp.bfloat16)
 
+    parrive(BY, lambda: (1, z, yy(-1)))
+    psend(BY + 2, lambda: (1, z, yy(-1)), lambda: ydev(1))
+    b_start(1)
+    parrive(BY + 1, lambda: (1, z, yy(1)))
+    b_start(2)
     k1_arrive(1)
     k1_arrive(2)
     k1_arrive(3)
@@ -244,8 +269,13 @@
     for n in (2, 6, 3, 7):
         send_q(n, row_h[n])
     send_q(1, x * 2 + 1 - core)
+    parrive(BY + 2, lambda: (1, z, yy(-2)))
+    b_start(3)
     k1_forward(1)
     k1_forward(2)
+    for i in range(3):
+        b_arrive(i, 3)
+        b_arrive(i, 4)
     k1_arrive(5)
     k1_arrive(6)
     k1_arrive(7)
@@ -254,6 +284,11 @@
     k1_forward(5)
     k1_forward(6)
     k1_forward(7)
+    b_arrive(3, 3)
+    b_arrive(3, 4)
+    for i in range(4):
+        for m in (1, 2, 5, 6, 7):
+            b_arrive(i, m)
     for n in range(8):
         parrive(YS + n, lambda n=n: (0, zz(zorder[n]), yy(1)))
     for n in range(8):
@@ -419,8 +454,8 @@
             dma((16,)),
             dma((1,)),
             dma((1,)),
-            dma((32,)),
-            dma((32,)),
+            dma((63,)),
+            dma((63,)),
         ],
         compiler_params=pltpu.CompilerParams(
             collective_id=0, has_side_effects=True, vmem_limit_bytes=60 << 20

time: 70.4 us -> 68.7 us (0.976)
  Pallas kernels: 68.6 us -> 67 us
    pallas_call x1, Pallas kernels: 67.2 us -> 65.6 us  [per_device(): pl.pallas_call(kernel, out_shape=shape, in_specs=[smem, smem, smem, smem,...]
where the time goes in v3:
time: 68.7 us; the launch traced here: 68.6 us
  Pallas kernels  67 us (98%)
  local copies, waits for them, and re-layouts  1.58 us (2%)
    pallas_call x1, Pallas kernels, per_device(): pl.pallas_call(kernel, out_shape=shape, in_specs=[smem, smem, smem, smem,...  65.6 us
    unnamed x2, local copies, waits for them, and re-layouts  1.58 us

profile of v3, /device:TPU:1, one launch (start us, length us, event | category | flops | bytes accessed | tf_op | source)
XLA Modules:
  0.0 68.6 jit_solution(9604531026845724370)
XLA Ops:
  0.0 65.6 %shard_map.82.src = bf16[1,128,8192]{2,1,0:T(8,128)(2,1)} custom-call(s32[1,1,2]{2,1,0:T(1,128)} %ids_ref.1, s32[1,32]{1,0:T(1,128)} %counts_ref.1, s32[4,8]{1,0:T(4,128)} %bitcast.6, s32[1,8]{1,0:T(1,128)} %bitcast.7, s32[8,64]{1,0:T(8,128)} %heads_ref.1, bf16[1,128,8192]{2,1,0:T(8,128)(2,1)} %q_ref.1, bf16[2,64,2048]{2,1,0:T(8,128)(2,1)} %bitcast.5, ...), custom_call_target="tpu_custom_call" | custom-call | flops 3221225472 | bytes 8388608 | tf_op jit(solution)/shard_map/pallas_call | solution.py:433
  65.6 0.0 copy-start
  65.6 1.6 %copy-done = bf16[1,128,8192]{2,1,0:T(8,128)(2,1)S(1)} copy-done((bf16[1,128,8192]{2,1,0:T(8,128)(2,1)S(1)}, bf16[1,128,8192]{2,1,0:T(8,128)(2,1)}, u32[]{:S(2)}) %copy-start) | copy-done | bytes 2097176
  67.2 1.4 %shard_map.83 = bf16[1,128,8192]{2,1,0:T(8,128)(2,1)} custom-call(bf16[1,128,8192]{2,1,0:T(8,128)(2,1)S(1)} %copy-done), custom_call_target="tpu_custom_call" | custom-call | tf_op jit(solution)/shard_map/pallas_call | solution.py:476
Async XLA Ops:
  65.6 1.6 %copy-start = (bf16[1,128,8192]{2,1,0:T(8,128)(2,1)S(1)}, bf16[1,128,8192]{2,1,0:T(8,128)(2,1)}, u32[]{:S(2)}) copy-start(bf16[1,128,8192]{2,1,0:T(8,128)(2,1)} %shard_map.82.src) | copy-start | bytes 6291460
